TPU v7x, 128 devices: a whole 4x4x4 slice. The times are simulated.
128 devices in a mesh: row: 8 (over y, x_hi), col: 16 (over z, x_lo, core).
Axes of the slice: x: 4 (x_hi: 2, x_lo: 2; x = x_hi * 2 + x_lo), y: 4, z: 4, core: 2. Of those that a mesh axis runs over, the one named last changes fastest.
Arguments:
- latent: float32 [8, 16, 256, 256], P(None, 'col', 'row'), may hold values from -6 to 6
- counts: int32 [16, 8, 256], P(None, 'row', 'col'), may hold values from 0 to 7
- baseline: float32 [16, 8, 256], P(None, 'row', 'col'), may hold values from -0.5 to 0.5
- tiles: float32 [8, 16, 72, 256, 256], P('row', 'col'), as said below
- tile_map: int32 [8, 16, 2, 72], P('row', 'col'), may hold values from -1 to 127, as said below
Outputs:
- latent_field: float32 [16, 8, 256, 256], P(None, 'row', 'col')
- gradient: float32 [8, 16, 256, 256], P(None, 'col', 'row')
Inputs may be any that keep to these rules, and one draw needn't show every extreme that they name: `tile_map`: for the device at row index p and col index q the slots list, in some order and each once, every block pair (i, j) with i >= j, i % 8 == p and j % 16 == q; the remaining slots hold -1 in both entries. The device at row 7, col 0 has no empty slot. tiles[p, q, s] is the tile of L named by tile_map[p, q, :, s]; where i = j it is lower triangular with a diagonal between 0.3 and 0.6; empty slots are zero.
All inputs are finite; a program needn't handle non-finite values.
Results may differ from a plain program's by a relative error of at most 0.0001.
Values sent between devices are 32-bit elements; how exact they have to be, the bound alone decides.
No kernel may reach another device: no remote copies, remote signals or barrier semaphores. Data moves between devices by JAX's collectives and lax.ppermute only.
A program may use at most 128 MiB of HBM per device.

v0:
```python
import jax
import jax.numpy as jnp
from jax import lax
from jax.experimental import pallas as pl
from jax.experimental.pallas import tpu as pltpu
from jax.sharding import PartitionSpec as P

F32 = jnp.float32
BF16 = jnp.bfloat16
TILE = 256
ROWS = 16
COLS = 8
PAIRS = [(a, b) for a in range(ROWS) for b in range(a // 2 + 1)]
INDEX = {pair: k for k, pair in enumerate(PAIRS)}
HELD = 18
DOT_ROWS = 128
SENT = {6: (0, 0), 5: (0, 1), 7: (0, 2), 4: (1, 0), 0: (1, 1), 1: (1, 2), 2: (1, 3), 3: (1, 4)}
SENT_SIZES = (3, 5)


def row_shift(x, dy, dx):
    pairs = [(i, (i // 2 + dy) % 4 * 2 + (i + dx) % 2) for i in range(8)]
    return lax.ppermute(x, "row", pairs)


def col_shift(x, dz, dx, dc):
    pairs = [
        (i, (i // 4 + dz) % 4 * 4 + (i // 2 + dx) % 2 * 2 + (i + dc) % 2)
        for i in range(16)
    ]
    return lax.ppermute(x, "col", pairs)


def split(x):
    high = x.astype(BF16)
    return high, (x - high.astype(F32)).astype(BF16)


def pack_kernel(begin, end, place, tile_map, tiles, *refs):
    out, held, sems = refs[-3:]

    def fetch(s, n):
        return pltpu.make_async_copy(tiles.at[0, 0, s], held.at[n], sems.at[n])

    for n in range(HELD):
        fetch(begin + n, n).start()
    if begin == 0:
        for b in range(COLS):
            for a in (2 * b, 2 * b + 1):

                @pl.when(8 * a + place[0] < 16 * b + place[1])
                def _():
                    out[INDEX[a, b]] = jnp.zeros(out.shape[1:], BF16)

    @pl.loop(begin, end, step=HELD)
    def _(first):
        for n in range(HELD):
            s = first + n
            fetch(s, n).wait()
            row = tile_map[0, s]

            @pl.when(row >= 0)
            def _():
                a = lax.shift_right_logical(row, 3)
                m = lax.shift_right_logical(a, 1)
                b = lax.shift_right_logical(tile_map[1, s], 4)
                k = m * (m + 1) + jnp.bitwise_and(a, 1) * (m + 1) + b
                out[k, 0], out[k, 1] = split(held[n])

            @pl.when(s + HELD < end)
            def _():
                fetch(s + HELD, n).start()


def pack(begin, end, place, tile_map, tiles, *begun):
    smem = pl.BlockSpec(memory_space=pltpu.SMEM)
    vmem = pl.BlockSpec(memory_space=pltpu.VMEM)
    return pl.pallas_call(
        lambda *refs: pack_kernel(begin, end, *refs),
        out_shape=jax.ShapeDtypeStruct((len(PAIRS), 2, TILE, TILE), BF16),
        in_specs=[smem, smem, pl.BlockSpec(memory_space=pltpu.HBM)] + [vmem] * len(begun),
        out_specs=vmem,
        input_output_aliases={3: 0} if begun else {},
        scratch_shapes=[
            pltpu.VMEM((HELD, TILE, TILE), F32),
            pltpu.SemaphoreType.DMA((HELD,)),
        ],
        compiler_params=pltpu.CompilerParams(vmem_limit_bytes=29 * 2**20),
        cost_estimate=pl.CostEstimate(
            flops=0, bytes_accessed=(end - begin) * TILE * TILE * 8, transcendentals=0
        ),
    )(place, tile_map, tiles, *begun)


def col_place(q, dc, dx, dz):
    z, x, c = q // 4, q // 2 % 2, q % 2
    return lax.rem(z + dz, 4) * 4 + lax.rem(x + dx, 2) * 2 + lax.rem(c + dc, 2)


def row_place(p, dx, dy):
    return lax.rem(p // 2 + dy, 4) * 2 + lax.rem(p % 2 + dx, 2)


def tile(packed, a, b):
    return packed.at[INDEX[a, b]]


def field_kernel(dc, place, *refs):
    pieces, packed, outs = refs[:8], refs[8], refs[9:-2]
    high, low = refs[-2:]
    p, q = place[0], place[1]
    chains = high.shape[-1]
    for n in range(8):
        start = pl.multiple_of(row_place(p, n // 4, 4 - n % 4) * 32, 32)
        high[:, pl.ds(start, 32), :], low[:, pl.ds(start, 32), :] = split(pieces[n][...])
    starts = [pl.multiple_of(col_place(q, dc, n // 4, n % 4) * 16, 16) for n in range(8)]

    def rows_of(a, b, part):
        chosen = tile(packed, a, b).at[part]
        return jnp.concatenate([chosen[pl.ds(start, 16), :] for start in starts], axis=0)

    for a in range(ROWS):
        count = a // 2 + 1
        h = high[:count].reshape(-1, chains)
        l = low[:count].reshape(-1, chains)
        right = jnp.concatenate([h, l, h], axis=0)
        tall = [rows_of(a, b, 0) for b in range(count)]
        rest = [rows_of(a, b, 1) for b in range(count)]
        left = jnp.concatenate(rest + tall + tall, axis=1)
        total = jnp.dot(left, right, preferred_element_type=F32)
        for n in range(8):
            part = total[16 * n : 16 * n + 16]
            if dc:
                group, member = SENT[n]
                outs[group][member, a] = part
            else:
                outs[n][a] = part


def gradient_kernel(dc, place, *refs):
    pieces, packed, partial, outs = refs[:8], refs[8], refs[9], refs[10:18]
    high, low = refs[18:20] if dc else refs[10:12]
    p, q = place[0], place[1]
    starts = [
        pl.multiple_of(col_place(q, dc, n // 4, 4 - n % 4) * 16, 16) for n in range(8)
    ]

    def rows_of(a, b, part):
        chosen = tile(packed, a, b).at[part]
        return jnp.concatenate([chosen[pl.ds(start, 16), :] for start in starts], axis=0)

    for a in range(ROWS):
        block = jnp.concatenate([piece[a] for piece in pieces], axis=0)
        high[a], low[a] = split(block.T)
    for b in range(COLS):
        blocks = range(2 * b, ROWS)
        tall = [rows_of(a, b, 0) for a in blocks]
        rest = [rows_of(a, b, 1) for a in blocks]
        right = jnp.concatenate(tall + rest + tall, axis=0)
        for begin in range(0, TILE, DOT_ROWS):
            rows = slice(begin, begin + DOT_ROWS)
            h = [high[a, rows] for a in blocks]
            l = [low[a, rows] for a in blocks]
            left = jnp.concatenate(l + h + h, axis=1)
            term = jnp.dot(left, right, preferred_element_type=F32)
            if dc:
                refs[20][b, :, rows] = (partial[b, rows] + term).T
            else:
                partial[b, rows] = term
    if dc:
        total = refs[20]
        for n in range(8):
            start = pl.multiple_of(row_place(p, n // 4, n % 4) * 32, 32)
            outs[n][...] = total[:, pl.ds(start, 32), :]


def call(kernel, place, operands, outs, scratch):
    vmem = pl.BlockSpec(memory_space=pltpu.VMEM)
    chains = outs[0][-1]
    count = len(PAIRS)
    return pl.pallas_call(
        kernel,
        out_shape=[jax.ShapeDtypeStruct(s, F32) for s in outs],
        in_specs=[pl.BlockSpec(memory_space=pltpu.SMEM)] + [vmem] * len(operands),
        out_specs=[vmem] * len(outs),
        scratch_shapes=scratch,
        compiler_params=pltpu.CompilerParams(vmem_limit_bytes=20 * 2**20),
        cost_estimate=pl.CostEstimate(
            flops=6 * count * TILE * TILE * chains,
            bytes_accessed=count * TILE * TILE * 4,
            transcendentals=0,
        ),
    )(place, *operands)


def field_product(dc, place, latent_pieces, packed):
    chains = latent_pieces[0].shape[-1]
    part = (ROWS, 16, chains)
    return call(
        lambda *refs: field_kernel(dc, *refs), place, [*latent_pieces, packed],
        [(size,) + part for size in SENT_SIZES] if dc else [part] * 8,
        [
            pltpu.VMEM((COLS, TILE, chains), BF16),
            pltpu.VMEM((COLS, TILE, chains), BF16),
        ],
    )


def gradient_product(dc, place, operands):
    chains = operands[0].shape[-1]
    scratch = [pltpu.VMEM((ROWS, chains, DOT_ROWS), BF16)] * 2
    if dc:
        scratch += [pltpu.VMEM((COLS, TILE, chains), F32)]
    return call(
        lambda *refs: gradient_kernel(dc, *refs), place, operands,
        [(COLS, 32, chains)] * 8 if dc else [(COLS, chains, TILE)],
        scratch,
    )


def gather(x, ring, flip, before=None):
    other = flip(x)
    far = ring(x, 2)
    near = [ring(x, 1), ring(x, 3)]
    if before is not None:
        other, before = lax.optimization_barrier((other, before))
    far, late = lax.optimization_barrier((far, other))
    across = [ring(other, 1), ring(late, 3)]
    return [x, near[0], far, near[1], other, across[0], flip(far), across[1]], before


def scatter_sum(parts, ring, flip):
    joined = parts[2] + flip(parts[6])
    across = parts[4] + ring(parts[5], 1) + ring(parts[7], 3)
    here = parts[0] + ring(parts[1], 1) + ring(parts[3], 3) + ring(joined, 2)
    return here + flip(across)


def body(latent, counts, baseline, tiles, tile_map):
    p, q = lax.axis_index("row"), lax.axis_index("col")
    place = jnp.stack([p, q]).astype(jnp.int32)
    noise = latent[:, 0]

    def ring_y(x, d):
        return row_shift(x, d, 0)

    def flip_y(x):
        return row_shift(x, 0, 1)

    def ring_z(x, d):
        return col_shift(x, d, 0, 0)

    def flip_z(x):
        return col_shift(x, 0, 1, 0)

    def swap(x):
        return col_shift(x, 0, 0, 1)

    with jax.named_scope("gather_latent"):
        half = len(PAIRS) // 2
        packed = pack(0, half, place, tile_map[0, 0], tiles)
        latent_pieces, packed = gather(noise, ring_y, flip_y, packed)
        packed = pack(half, 2 * half, place, tile_map[0, 0], tiles, packed)
    with jax.named_scope("field_product"):
        sent = field_product(1, place, latent_pieces, packed)
        after, _ = lax.optimization_barrier((place, sent[0]))
        keep = field_product(0, after, latent_pieces, packed)
    with jax.named_scope("reduce_field"):
        other = [swap(s) for s in sent]
        paired = {}
        for group in range(len(sent)):
            members = [n for n in SENT if SENT[n][0] == group]
            sums = [keep[n] + other[group][SENT[n][1]] for n in members]
            paired.update(zip(members, lax.optimization_barrier(sums)))
        field = scatter_sum(paired, ring_z, flip_z)
    count = counts[:, 0].astype(F32)[..., None]
    slope = count - jnp.exp(baseline[:, 0][..., None] + field)
    with jax.named_scope("gather_slope"):
        slope_pieces, _ = gather(slope, ring_z, flip_z)
        ready = dict(enumerate(slope_pieces))
        first = (0, 4, 1, 3, 2, 5)
        ready.update(zip(first, lax.optimization_barrier([ready[n] for n in first])))
        swapped = [swap(ready[n]) for n in range(8)]
    with jax.named_scope("gradient_product"):
        (partial,) = gradient_product(0, place, [*slope_pieces, packed])
        parts = gradient_product(1, place, [*swapped, packed, partial])
    with jax.named_scope("reduce_gradient"):
        gradient = noise - scatter_sum(parts, ring_y, flip_y)
    return (field[:, None], gradient[:, None])


def solution(mesh):
    return jax.shard_map(
        body,
        mesh=mesh,
        in_specs=(
            P(None, "col", "row", None),
            P(None, "row", "col"),
            P(None, "row", "col"),
            P("row", "col", None, None, None),
            P("row", "col", None, None),
        ),
        out_specs=(P(None, "row", "col", None), P(None, "col", "row", None)),
        check_vma=False,
    )
```

profile of v0, /device:TPU:1, one launch (start us, length us, event | category | flops | bytes accessed | tf_op | source)
XLA Modules:
  0.0 120.0 jit_solution(13905749087256932070)
XLA Ops:
  0.6 3.7 %collective-permute-start.2 = (f32[8,32,256]{2,1,0:T(8,128)}, f32[8,32,256]{2,1,0:T(8,128)S(1)}, u32[]{:S(2)}, u32[]{:S(2)}) collective-permute-start(f32[8,32,256]{2,1,0:T(8,128)} %bitcast.46), channel_id=1, source_target_pairs={{0,16},{16,0},{32,48},{48,32},{64,80},{80,64},{96,112},{112,96},{1... | collective-permute-start | bytes 786440 | tf_op jit(solution)/shard_map/gather_latent/ppermute | solution.py:23
  4.3 2.9 %collective-permute-start.1 = (f32[8,32,256]{2,1,0:T(8,128)}, f32[8,32,256]{2,1,0:T(8,128)S(1)}, u32[]{:S(2)}, u32[]{:S(2)}) collective-permute-start(f32[8,32,256]{2,1,0:T(8,128)} %bitcast.47), channel_id=1, source_target_pairs={{0,64},{16,80},{32,96},{48,112},{64,0},{80,16},{96,32},{112,48},{1... | collective-permute-start | bytes 786440 | tf_op jit(solution)/shard_map/gather_latent/ppermute | solution.py:23
  7.6 2.3 %collective-permute-start.3 = (f32[8,32,256]{2,1,0:T(8,128)}, f32[8,32,256]{2,1,0:T(8,128)S(1)}, u32[]{:S(2)}, u32[]{:S(2)}) collective-permute-start(f32[8,32,256]{2,1,0:T(8,128)} %bitcast.49), channel_id=1, source_target_pairs={{0,96},{16,112},{32,0},{48,16},{64,32},{80,48},{96,64},{112,80},{1... | collective-permute-start | bytes 786440 | tf_op jit(solution)/shard_map/gather_latent/ppermute | solution.py:23
  10.6 4.6 %gather_latent.2.refs_3_ = bf16[72,2,256,256]{3,2,1,0:T(8,128)(2,1)S(1)} custom-call(s32[2]{0:T(128)S(1)} %pad_add_fusion.refs_0_, s32[2,72]{1,0:T(2,128)S(1)} %bitcast.52, f32[1,1,72,256,256]{4,3,2,1,0:T(8,128)} %refs_2_.3), custom_call_target="tpu_custom_call" | custom-call | bytes 18874368 | tf_op jit(solution)/shard_map/gather_latent/pallas_call | solution.py:78
  17.1 4.6 %gather_latent.3.refs_9_ = bf16[72,2,256,256]{3,2,1,0:T(8,128)(2,1)S(1)} custom-call(s32[2]{0:T(128)S(1)} %pad_add_fusion.refs_0_, s32[2,72]{1,0:T(2,128)S(1)} %bitcast.53, f32[1,1,72,256,256]{4,3,2,1,0:T(8,128)} %refs_2_.3, bf16[72,2,256,256]{3,2,1,0:T(8,128)(2,1)S(1)} %gather_latent.2.refs_3_), custom_call_target="tpu_custom_call", output_to_operand_aliasing={{}: (3, {})} | custom-call | bytes 18874368 | tf_op jit(solution)/shard_map/gather_latent/pallas_call | solution.py:78
  24.4 4.8 %field_product.2 = (f32[3,16,16,256]{3,2,1,0:T(8,128)S(1)}, f32[5,16,16,256]{3,2,1,0:T(8,128)S(1)}) custom-call(s32[2]{0:T(128)S(1)} %pad_add_fusion.refs_0_, f32[8,32,256]{2,1,0:T(8,128)S(1)} %bitcast.50, f32[8,32,256]{2,1,0:T(8,128)S(1)} %collective-permute-done.refs_2_, f32[8,32,256]{2,1,0:T(8,128)S(1)} %collective-permute-done.1.refs_3_, ...), custom_call_target="tpu_custom_call" | custom-call | flops 7247757312 | bytes 18874368 | tf_op jit(solution)/shard_map/field_product/pallas_call | solution.py:181
  29.3 2.9 %collective-permute-start.7 = (f32[5,16,16,256]{3,2,1,0:T(8,128)S(1)}, f32[5,16,16,256]{3,2,1,0:T(8,128)S(1)}, u32[]{:S(2)}, u32[]{:S(2)}) collective-permute-start(f32[5,16,16,256]{3,2,1,0:T(8,128)S(1)} %get-tuple-element.48), channel_id=1, source_target_pairs={{0,1},{1,0},{2,3},{3,2},{4,5},{5,4},{6,7},{7,6},{8,9},{9,8},{10,11... | collective-permute-start | bytes 3932168 | tf_op jit(solution)/shard_map/reduce_field/ppermute | solution.py:31
  32.5 4.8 %field_product.3 = (f32[16,16,256]{2,1,0:T(8,128)S(1)}, f32[16,16,256]{2,1,0:T(8,128)S(1)}, f32[16,16,256]{2,1,0:T(8,128)S(1)}, f32[16,16,256]{2,1,0:T(8,128)S(1...) custom-call(s32[2]{0:T(128)S(1)} %pad_add_fusion.refs_0_, ...), custom_call_target="tpu_custom_call" | custom-call | flops 7247757312 | bytes 18874368 | tf_op jit(solution)/shard_map/field_product/pallas_call | solution.py:181
  39.1 1.6 %collective-permute-start.13 = (f32[16,16,256]{2,1,0:T(8,128)S(1)}, f32[16,16,256]{2,1,0:T(8,128)S(1)}, u32[]{:S(2)}, u32[]{:S(2)}) collective-permute-start(f32[16,16,256]{2,1,0:T(8,128)S(1)} %get-tuple-element.62), channel_id=1, source_target_pairs={{0,4},{1,5},{2,6},{3,7},{4,8},{5,9},{6,10},{7,11},{8,12},{9,13},{1... | collective-permute-start | bytes 786440 | tf_op jit(solution)/shard_map/reduce_field/ppermute | solution.py:31
  40.8 2.1 %collective-permute-start.14 = (f32[16,16,256]{2,1,0:T(8,128)S(1)}, f32[16,16,256]{2,1,0:T(8,128)S(1)}, u32[]{:S(2)}, u32[]{:S(2)}) collective-permute-start(f32[16,16,256]{2,1,0:T(8,128)S(1)} %get-tuple-element.63), channel_id=1, source_target_pairs={{0,12},{1,13},{2,14},{3,15},{4,0},{5,1},{6,2},{7,3},{8,4},{9,5},{1... | collective-permute-start | bytes 786440 | tf_op jit(solution)/shard_map/reduce_field/ppermute | solution.py:31
  42.9 2.7 %collective-permute-start.9 = (f32[16,16,256]{2,1,0:T(8,128)S(1)}, f32[16,16,256]{2,1,0:T(8,128)S(1)}, u32[]{:S(2)}, u32[]{:S(2)}) collective-permute-start(f32[16,16,256]{2,1,0:T(8,128)S(1)} %get-tuple-element.55), channel_id=1, source_target_pairs={{0,12},{1,13},{2,14},{3,15},{4,0},{5,1},{6,2},{7,3},{8,4},{9,5},{1... | collective-permute-start | bytes 786440 | tf_op jit(solution)/shard_map/reduce_field/ppermute | solution.py:31
  45.6 3.7 %collective-permute-start.12 = (f32[16,16,256]{2,1,0:T(8,128)S(1)}, f32[16,16,256]{2,1,0:T(8,128)S(1)}, u32[]{:S(2)}, u32[]{:S(2)}) collective-permute-start(f32[16,16,256]{2,1,0:T(8,128)S(1)} %add.86), channel_id=1, source_target_pairs={{0,8},{1,9},{2,10},{3,11},{4,12},{5,13},{6,14},{7,15},{8,0},{9,1},... | collective-permute-start | bytes 786440 | tf_op jit(solution)/shard_map/reduce_field/ppermute | solution.py:31
  50.7 4.0 %collective-permute-done.8 = f32[16,16,256]{2,1,0:T(8,128)S(1)} collective-permute-done((f32[16,16,256]{2,1,0:T(8,128)S(1)}, f32[16,16,256]{2,1,0:T(8,128)S(1)}, u32[]{:S(2)}, u32[]{:S(2)}) %collective-permute-start.8) | collective-permute-done | bytes 262176 | tf_op jit(solution)/shard_map/reduce_field/ppermute | solution.py:31
  54.7 6.5 %collective-permute-done.12 = f32[16,16,256]{2,1,0:T(8,128)S(1)} collective-permute-done((f32[16,16,256]{2,1,0:T(8,128)S(1)}, f32[16,16,256]{2,1,0:T(8,128)S(1)}, u32[]{:S(2)}, u32[]{:S(2)}) %collective-permute-start.12) | collective-permute-done | bytes 262176 | tf_op jit(solution)/shard_map/reduce_field/ppermute | solution.py:31
  63.5 1.7 %collective-permute-start.18 = (f32[16,16,256]{2,1,0:T(8,128)S(1)}, f32[16,16,256]{2,1,0:T(8,128)S(1)}, u32[]{:S(2)}, u32[]{:S(2)}) collective-permute-start(f32[16,16,256]{2,1,0:T(8,128)S(1)} %get-tuple-element.65.refs_1_), channel_id=1, source_target_pairs={{0,12},{1,13},{2,14},{3,15},{4,0},{5,1},{6,2},{7,3},{8,4},{9,5},{1... | collective-permute-start | bytes 786440 | tf_op jit(solution)/shard_map/gather_slope/ppermute | solution.py:31
  65.2 3.2 %collective-permute-done.16.refs_5_ = f32[16,16,256]{2,1,0:T(8,128)S(1)} collective-permute-done((f32[16,16,256]{2,1,0:T(8,128)S(1)}, f32[16,16,256]{2,1,0:T(8,128)S(1)}, u32[]{:S(2)}, u32[]{:S(2)}) %collective-permute-start.16) | collective-permute-done | bytes 262176 | tf_op jit(solution)/shard_map/gather_slope/ppermute | solution.py:31
  71.4 6.2 %collective-permute-done.17.refs_2_ = f32[16,16,256]{2,1,0:T(8,128)S(1)} collective-permute-done((f32[16,16,256]{2,1,0:T(8,128)S(1)}, f32[16,16,256]{2,1,0:T(8,128)S(1)}, u32[]{:S(2)}, u32[]{:S(2)}) %collective-permute-start.17) | collective-permute-done | bytes 262176 | tf_op jit(solution)/shard_map/gather_slope/ppermute | solution.py:31
  77.5 5.6 %collective-permute-done.20.refs_6_ = f32[16,16,256]{2,1,0:T(8,128)S(1)} collective-permute-done((f32[16,16,256]{2,1,0:T(8,128)S(1)}, f32[16,16,256]{2,1,0:T(8,128)S(1)}, u32[]{:S(2)}, u32[]{:S(2)}) %collective-permute-start.20) | collective-permute-done | bytes 262176 | tf_op jit(solution)/shard_map/gather_slope/ppermute | solution.py:31
  86.0 5.0 %gradient_product.2.refs_10_ = f32[8,256,256]{2,1,0:T(8,128)S(1)} custom-call(s32[2]{0:T(128)S(1)} %pad_add_fusion.refs_0_, f32[16,16,256]{2,1,0:T(8,128)S(1)} %get-tuple-element.65.refs_1_, f32[16,16,256]{2,1,0:T(8,128)S(1)} %collective-permute-done.17.refs_2_, f32[16,16,256]{2,1,0:T(8,128)S(1)} %collective-permute-done.19.refs_3_, ...), custom_call_target="tpu_custom_call" | custom-call | flops 7247757312 | bytes 18874368 | tf_op jit(solution)/shard_map/gradient_product/pallas_call | solution.py:181
  91.0 5.4 %gradient_product.3 = (f32[8,32,256]{2,1,0:T(8,128)S(1)}, f32[8,32,256]{2,1,0:T(8,128)S(1)}, f32[8,32,256]{2,1,0:T(8,128)S(1)}, f32[8,32,256]{2,1,0:T(8,128)S(1)...) custom-call(s32[2]{0:T(128)S(1)} %pad_add_fusion.refs_0_, ...), custom_call_target="tpu_custom_call" | custom-call | flops 7247757312 | bytes 18874368 | tf_op jit(solution)/shard_map/gradient_product/pallas_call | solution.py:181
  96.4 2.8 %collective-permute-start.33 = (f32[8,32,256]{2,1,0:T(8,128)S(1)}, f32[8,32,256]{2,1,0:T(8,128)S(1)}, u32[]{:S(2)}, u32[]{:S(2)}) collective-permute-start(f32[8,32,256]{2,1,0:T(8,128)S(1)} %get-tuple-element.76), channel_id=1, source_target_pairs={{0,16},{16,0},{32,48},{48,32},{64,80},{80,64},{96,112},{112,96},{1... | collective-permute-start | bytes 786440 | tf_op jit(solution)/shard_map/reduce_gradient/ppermute | solution.py:23
  99.3 2.7 %collective-permute-start.36 = (f32[8,32,256]{2,1,0:T(8,128)S(1)}, f32[8,32,256]{2,1,0:T(8,128)S(1)}, u32[]{:S(2)}, u32[]{:S(2)}) collective-permute-start(f32[8,32,256]{2,1,0:T(8,128)S(1)} %get-tuple-element.79), channel_id=1, source_target_pairs={{0,96},{16,112},{32,0},{48,16},{64,32},{80,48},{96,64},{112,80},{1... | collective-permute-start | bytes 786440 | tf_op jit(solution)/shard_map/reduce_gradient/ppermute | solution.py:23
  101.9 2.7 %collective-permute-start.32 = (f32[8,32,256]{2,1,0:T(8,128)S(1)}, f32[8,32,256]{2,1,0:T(8,128)S(1)}, u32[]{:S(2)}, u32[]{:S(2)}) collective-permute-start(f32[8,32,256]{2,1,0:T(8,128)S(1)} %get-tuple-element.74), channel_id=1, source_target_pairs={{0,96},{16,112},{32,0},{48,16},{64,32},{80,48},{96,64},{112,80},{1... | collective-permute-start | bytes 786440 | tf_op jit(solution)/shard_map/reduce_gradient/ppermute | solution.py:23
  108.8 10.3 %collective-permute-done.31 = f32[8,32,256]{2,1,0:T(8,128)S(1)} collective-permute-done((f32[8,32,256]{2,1,0:T(8,128)S(1)}, f32[8,32,256]{2,1,0:T(8,128)S(1)}, u32[]{:S(2)}, u32[]{:S(2)}) %collective-permute-start.31) | collective-permute-done | bytes 262176 | tf_op jit(solution)/shard_map/reduce_gradient/ppermute | solution.py:23
  (75 shorter events, 22.3 us)
Async XLA Ops:
  0.6 14.7 %collective-permute-start.2 = (f32[8,32,256]{2,1,0:T(8,128)}, f32[8,32,256]{2,1,0:T(8,128)S(1)}, u32[]{:S(2)}, u32[]{:S(2)}) collective-permute-start(f32[8,32,256]{2,1,0:T(8,128)} %bitcast.46), channel_id=1, source_target_pairs={{0,16},{16,0},{32,48},{48,32},{64,80},{80,64},{96,112},{112,96},{1... | collective-permute-start | bytes 786440 | tf_op jit(solution)/shard_map/gather_latent/ppermute | solution.py:23
  4.3 11.0 %collective-permute-start.1 = (f32[8,32,256]{2,1,0:T(8,128)}, f32[8,32,256]{2,1,0:T(8,128)S(1)}, u32[]{:S(2)}, u32[]{:S(2)}) collective-permute-start(f32[8,32,256]{2,1,0:T(8,128)} %bitcast.47), channel_id=1, source_target_pairs={{0,64},{16,80},{32,96},{48,112},{64,0},{80,16},{96,32},{112,48},{1... | collective-permute-start | bytes 786440 | tf_op jit(solution)/shard_map/gather_latent/ppermute | solution.py:23
  7.2 14.5 %collective-permute-start = (f32[8,32,256]{2,1,0:T(8,128)}, f32[8,32,256]{2,1,0:T(8,128)S(1)}, u32[]{:S(2)}, u32[]{:S(2)}) collective-permute-start(f32[8,32,256]{2,1,0:T(8,128)} %bitcast.48), channel_id=1, source_target_pairs={{0,32},{16,48},{32,64},{48,80},{64,96},{80,112},{96,0},{112,16},{1... | collective-permute-start | bytes 786440 | tf_op jit(solution)/shard_map/gather_latent/ppermute | solution.py:23
  7.6 14.1 %collective-permute-start.3 = (f32[8,32,256]{2,1,0:T(8,128)}, f32[8,32,256]{2,1,0:T(8,128)S(1)}, u32[]{:S(2)}, u32[]{:S(2)}) collective-permute-start(f32[8,32,256]{2,1,0:T(8,128)} %bitcast.49), channel_id=1, source_target_pairs={{0,96},{16,112},{32,0},{48,16},{64,32},{80,48},{96,64},{112,80},{1... | collective-permute-start | bytes 786440 | tf_op jit(solution)/shard_map/gather_latent/ppermute | solution.py:23
  15.6 8.8 %collective-permute-start.6 = (f32[8,32,256]{2,1,0:T(8,128)S(1)}, f32[8,32,256]{2,1,0:T(8,128)S(1)}, u32[]{:S(2)}, u32[]{:S(2)}) collective-permute-start(f32[8,32,256]{2,1,0:T(8,128)S(1)} %collective-permute-done.2.refs_5_), channel_id=1, source_target_pairs={{0,96},{16,112},{32,0},{48,16},{64,32},{80,48},{96,64},{112,80},{1... | collective-permute-start | bytes 786440 | tf_op jit(solution)/shard_map/gather_latent/ppermute | solution.py:23
  15.9 8.5 %collective-permute-start.4 = (f32[8,32,256]{2,1,0:T(8,128)S(1)}, f32[8,32,256]{2,1,0:T(8,128)S(1)}, u32[]{:S(2)}, u32[]{:S(2)}) collective-permute-start(f32[8,32,256]{2,1,0:T(8,128)S(1)} %collective-permute-done.2.refs_5_), channel_id=1, source_target_pairs={{0,32},{16,48},{32,64},{48,80},{64,96},{80,112},{96,0},{112,16},{1... | collective-permute-start | bytes 786440 | tf_op jit(solution)/shard_map/gather_latent/ppermute | solution.py:23
  39.1 10.2 %collective-permute-start.13 = (f32[16,16,256]{2,1,0:T(8,128)S(1)}, f32[16,16,256]{2,1,0:T(8,128)S(1)}, u32[]{:S(2)}, u32[]{:S(2)}) collective-permute-start(f32[16,16,256]{2,1,0:T(8,128)S(1)} %get-tuple-element.62), channel_id=1, source_target_pairs={{0,4},{1,5},{2,6},{3,7},{4,8},{5,9},{6,10},{7,11},{8,12},{9,13},{1... | collective-permute-start | bytes 786440 | tf_op jit(solution)/shard_map/reduce_field/ppermute | solution.py:31
  40.8 8.5 %collective-permute-start.14 = (f32[16,16,256]{2,1,0:T(8,128)S(1)}, f32[16,16,256]{2,1,0:T(8,128)S(1)}, u32[]{:S(2)}, u32[]{:S(2)}) collective-permute-start(f32[16,16,256]{2,1,0:T(8,128)S(1)} %get-tuple-element.63), channel_id=1, source_target_pairs={{0,12},{1,13},{2,14},{3,15},{4,0},{5,1},{6,2},{7,3},{8,4},{9,5},{1... | collective-permute-start | bytes 786440 | tf_op jit(solution)/shard_map/reduce_field/ppermute | solution.py:31
  42.9 11.8 %collective-permute-start.8 = (f32[16,16,256]{2,1,0:T(8,128)S(1)}, f32[16,16,256]{2,1,0:T(8,128)S(1)}, u32[]{:S(2)}, u32[]{:S(2)}) collective-permute-start(f32[16,16,256]{2,1,0:T(8,128)S(1)} %get-tuple-element.54), channel_id=1, source_target_pairs={{0,4},{1,5},{2,6},{3,7},{4,8},{5,9},{6,10},{7,11},{8,12},{9,13},{1... | collective-permute-start | bytes 786440 | tf_op jit(solution)/shard_map/reduce_field/ppermute | solution.py:31
  42.9 11.8 %collective-permute-start.9 = (f32[16,16,256]{2,1,0:T(8,128)S(1)}, f32[16,16,256]{2,1,0:T(8,128)S(1)}, u32[]{:S(2)}, u32[]{:S(2)}) collective-permute-start(f32[16,16,256]{2,1,0:T(8,128)S(1)} %get-tuple-element.55), channel_id=1, source_target_pairs={{0,12},{1,13},{2,14},{3,15},{4,0},{5,1},{6,2},{7,3},{8,4},{9,5},{1... | collective-permute-start | bytes 786440 | tf_op jit(solution)/shard_map/reduce_field/ppermute | solution.py:31
  45.6 15.6 %collective-permute-start.12 = (f32[16,16,256]{2,1,0:T(8,128)S(1)}, f32[16,16,256]{2,1,0:T(8,128)S(1)}, u32[]{:S(2)}, u32[]{:S(2)}) collective-permute-start(f32[16,16,256]{2,1,0:T(8,128)S(1)} %add.86), channel_id=1, source_target_pairs={{0,8},{1,9},{2,10},{3,11},{4,12},{5,13},{6,14},{7,15},{8,0},{9,1},... | collective-permute-start | bytes 786440 | tf_op jit(solution)/shard_map/reduce_field/ppermute | solution.py:31
  49.4 11.8 %collective-permute-start.15 = (f32[16,16,256]{2,1,0:T(8,128)S(1)}, f32[16,16,256]{2,1,0:T(8,128)S(1)}, u32[]{:S(2)}, u32[]{:S(2)}) collective-permute-start(f32[16,16,256]{2,1,0:T(8,128)S(1)} %add_add_fusion.1), channel_id=1, source_target_pairs={{0,2},{1,3},{2,0},{3,1},{4,6},{5,7},{6,4},{7,5},{8,10},{9,11},{10,... | collective-permute-start | bytes 786440 | tf_op jit(solution)/shard_map/reduce_field/ppermute | solution.py:31
  62.3 15.3 %collective-permute-start.17 = (f32[16,16,256]{2,1,0:T(8,128)S(1)}, f32[16,16,256]{2,1,0:T(8,128)S(1)}, u32[]{:S(2)}, u32[]{:S(2)}) collective-permute-start(f32[16,16,256]{2,1,0:T(8,128)S(1)} %get-tuple-element.65.refs_1_), channel_id=1, source_target_pairs={{0,4},{1,5},{2,6},{3,7},{4,8},{5,9},{6,10},{7,11},{8,12},{9,13},{1... | collective-permute-start | bytes 786440 | tf_op jit(solution)/shard_map/gather_slope/ppermute | solution.py:31
  63.5 14.0 %collective-permute-start.18 = (f32[16,16,256]{2,1,0:T(8,128)S(1)}, f32[16,16,256]{2,1,0:T(8,128)S(1)}, u32[]{:S(2)}, u32[]{:S(2)}) collective-permute-start(f32[16,16,256]{2,1,0:T(8,128)S(1)} %get-tuple-element.65.refs_1_), channel_id=1, source_target_pairs={{0,12},{1,13},{2,14},{3,15},{4,0},{5,1},{6,2},{7,3},{8,4},{9,5},{1... | collective-permute-start | bytes 786440 | tf_op jit(solution)/shard_map/gather_slope/ppermute | solution.py:31
  68.4 14.7 %collective-permute-start.20 = (f32[16,16,256]{2,1,0:T(8,128)S(1)}, f32[16,16,256]{2,1,0:T(8,128)S(1)}, u32[]{:S(2)}, u32[]{:S(2)}) collective-permute-start(f32[16,16,256]{2,1,0:T(8,128)S(1)} %collective-permute-done.16.refs_5_), channel_id=1, source_target_pairs={{0,4},{1,5},{2,6},{3,7},{4,8},{5,9},{6,10},{7,11},{8,12},{9,13},{1... | collective-permute-start | bytes 786440 | tf_op jit(solution)/shard_map/gather_slope/ppermute | solution.py:31
  70.0 14.2 %collective-permute-start.27 = (f32[16,16,256]{2,1,0:T(8,128)S(1)}, f32[16,16,256]{2,1,0:T(8,128)S(1)}, u32[]{:S(2)}, u32[]{:S(2)}) collective-permute-start(f32[16,16,256]{2,1,0:T(8,128)S(1)} %collective-permute-done.19.refs_3_), channel_id=1, source_target_pairs={{0,2},{1,3},{2,0},{3,1},{4,6},{5,7},{6,4},{7,5},{8,10},{9,11},{10,... | collective-permute-start | bytes 786440 | tf_op jit(solution)/shard_map/gather_slope/ppermute | solution.py:31
  71.2 13.0 %collective-permute-start.29 = (f32[16,16,256]{2,1,0:T(8,128)S(1)}, f32[16,16,256]{2,1,0:T(8,128)S(1)}, u32[]{:S(2)}, u32[]{:S(2)}) collective-permute-start(f32[16,16,256]{2,1,0:T(8,128)S(1)} %collective-permute-done.16.refs_5_), channel_id=1, source_target_pairs={{0,12},{1,13},{2,14},{3,15},{4,0},{5,1},{6,2},{7,3},{8,4},{9,5},{1... | collective-permute-start | bytes 786440 | tf_op jit(solution)/shard_map/gather_slope/ppermute | solution.py:31
  96.4 9.4 %collective-permute-start.33 = (f32[8,32,256]{2,1,0:T(8,128)S(1)}, f32[8,32,256]{2,1,0:T(8,128)S(1)}, u32[]{:S(2)}, u32[]{:S(2)}) collective-permute-start(f32[8,32,256]{2,1,0:T(8,128)S(1)} %get-tuple-element.76), channel_id=1, source_target_pairs={{0,16},{16,0},{32,48},{48,32},{64,80},{80,64},{96,112},{112,96},{1... | collective-permute-start | bytes 786440 | tf_op jit(solution)/shard_map/reduce_gradient/ppermute | solution.py:23
  99.2 8.7 %collective-permute-start.35 = (f32[8,32,256]{2,1,0:T(8,128)S(1)}, f32[8,32,256]{2,1,0:T(8,128)S(1)}, u32[]{:S(2)}, u32[]{:S(2)}) collective-permute-start(f32[8,32,256]{2,1,0:T(8,128)S(1)} %get-tuple-element.78), channel_id=1, source_target_pairs={{0,32},{16,48},{32,64},{48,80},{64,96},{80,112},{96,0},{112,16},{1... | collective-permute-start | bytes 786440 | tf_op jit(solution)/shard_map/reduce_gradient/ppermute | solution.py:23
  99.3 8.7 %collective-permute-start.36 = (f32[8,32,256]{2,1,0:T(8,128)S(1)}, f32[8,32,256]{2,1,0:T(8,128)S(1)}, u32[]{:S(2)}, u32[]{:S(2)}) collective-permute-start(f32[8,32,256]{2,1,0:T(8,128)S(1)} %get-tuple-element.79), channel_id=1, source_target_pairs={{0,96},{16,112},{32,0},{48,16},{64,32},{80,48},{96,64},{112,80},{1... | collective-permute-start | bytes 786440 | tf_op jit(solution)/shard_map/reduce_gradient/ppermute | solution.py:23
  101.9 17.2 %collective-permute-start.31 = (f32[8,32,256]{2,1,0:T(8,128)S(1)}, f32[8,32,256]{2,1,0:T(8,128)S(1)}, u32[]{:S(2)}, u32[]{:S(2)}) collective-permute-start(f32[8,32,256]{2,1,0:T(8,128)S(1)} %get-tuple-element.73), channel_id=1, source_target_pairs={{0,32},{16,48},{32,64},{48,80},{64,96},{80,112},{96,0},{112,16},{1... | collective-permute-start | bytes 786440 | tf_op jit(solution)/shard_map/reduce_gradient/ppermute | solution.py:23
  101.9 17.2 %collective-permute-start.32 = (f32[8,32,256]{2,1,0:T(8,128)S(1)}, f32[8,32,256]{2,1,0:T(8,128)S(1)}, u32[]{:S(2)}, u32[]{:S(2)}) collective-permute-start(f32[8,32,256]{2,1,0:T(8,128)S(1)} %get-tuple-element.74), channel_id=1, source_target_pairs={{0,96},{16,112},{32,0},{48,16},{64,32},{80,48},{96,64},{112,80},{1... | collective-permute-start | bytes 786440 | tf_op jit(solution)/shard_map/reduce_gradient/ppermute | solution.py:23
  105.8 13.3 %collective-permute-start.34 = (f32[8,32,256]{2,1,0:T(8,128)S(1)}, f32[8,32,256]{2,1,0:T(8,128)S(1)}, u32[]{:S(2)}, u32[]{:S(2)}) collective-permute-start(f32[8,32,256]{2,1,0:T(8,128)S(1)} %add.96), channel_id=1, source_target_pairs={{0,64},{16,80},{32,96},{48,112},{64,0},{80,16},{96,32},{112,48},{1... | collective-permute-start | bytes 786440 | tf_op jit(solution)/shard_map/reduce_gradient/ppermute | solution.py:23
  108.0 11.2 %collective-permute-start.37 = (f32[8,32,256]{2,1,0:T(8,128)S(1)}, f32[8,32,256]{2,1,0:T(8,128)S(1)}, u32[]{:S(2)}, u32[]{:S(2)}) collective-permute-start(f32[8,32,256]{2,1,0:T(8,128)S(1)} %add_add_fusion), channel_id=1, source_target_pairs={{0,16},{16,0},{32,48},{48,32},{64,80},{80,64},{96,112},{112,96},{1... | collective-permute-start | bytes 786440 | tf_op jit(solution)/shard_map/reduce_gradient/ppermute | solution.py:23
  (18 other events, 125.7 us)
where the time goes:
time: 120 us
  starting transfers between devices  44.3 us (37%)
  waiting for transfers between devices  42.5 us (35%)
  Pallas kernels  29.2 us (24%)
  other arithmetic  2.4 us (2%)
    ppermute x24, waiting for transfers between devices, col_shift(): return lax.ppermute(x, 'col', pairs)  27 us
    ppermute x24, starting transfers between devices, col_shift(): return lax.ppermute(x, 'col', pairs)  23.4 us
    ppermute x14, starting transfers between devices, row_shift(): return lax.ppermute(x, 'row', pairs)  20.9 us
    pallas_call x4, Pallas kernels, call(): pl.pallas_call(kernel, out_shape=[jax.ShapeDtypeStruct(s, F32) for s in o...  20 us
    ppermute x14, waiting for transfers between devices, row_shift(): return lax.ppermute(x, 'row', pairs)  15.5 us
    pallas_call x2, Pallas kernels, pack(): pl.pallas_call(lambda *refs: pack_kernel(begin, end, *refs), out_shape=ja...  9.23 us
  transfers between devices with their start and end apart: 38, of which 12 were waited for; matrix products, arithmetic and copies ran while one was open for 0% of the time, Pallas kernels for 16%

commit v1 on v0

--- a/solution.py
+++ b/solution.py
@@ -16,6 +16,8 @@
 DOT_ROWS = 128
 SENT = {6: (0, 0), 5: (0, 1), 7: (0, 2), 4: (1, 0), 0: (1, 1), 1: (1, 2), 2: (1, 3), 3: (1, 4)}
 SENT_SIZES = (3, 5)
+MORE = COLS // 2
+GRADIENT_SIZES = (COLS, COLS - MORE, COLS, COLS - MORE, COLS, COLS + MORE, COLS, COLS + MORE)
 
 
 def row_shift(x, dy, dx):
@@ -171,7 +173,13 @@
         total = refs[20]
         for n in range(8):
             start = pl.multiple_of(row_place(p, n // 4, n % 4) * 32, 32)
-            outs[n][...] = total[:, pl.ds(start, 32), :]
+            part = total[:, pl.ds(start, 32), :]
+            if n in (1, 3):
+                outs[n + 4][COLS:], outs[n][...] = part[:MORE], part[MORE:]
+            elif n in (5, 7):
+                outs[n][:COLS] = part
+            else:
+                outs[n][...] = part
 
 
 def call(kernel, place, operands, outs, scratch):
@@ -213,7 +221,7 @@
         scratch += [pltpu.VMEM((COLS, TILE, chains), F32)]
     return call(
         lambda *refs: gradient_kernel(dc, *refs), place, operands,
-        [(COLS, 32, chains)] * 8 if dc else [(COLS, chains, TILE)],
+        [(size, 32, chains) for size in GRADIENT_SIZES] if dc else [(COLS, chains, TILE)],
         scratch,
     )
 
@@ -230,9 +238,14 @@
 
 
 def scatter_sum(parts, ring, flip):
+    size = parts[0].shape[0]
+    far = [ring(parts[5], 1), ring(parts[7], 3)]
+    across = parts[4] + far[0][:size] + far[1][:size]
     joined = parts[2] + flip(parts[6])
-    across = parts[4] + ring(parts[5], 1) + ring(parts[7], 3)
-    here = parts[0] + ring(parts[1], 1) + ring(parts[3], 3) + ring(joined, 2)
+    near = [ring(parts[1], 1), ring(parts[3], 3)]
+    if parts[1].shape[0] < size:
+        near = [jnp.concatenate([f[size:], n]) for f, n in zip(far, near)]
+    here = parts[0] + ring(joined, 2) + near[0] + near[1]
     return here + flip(across)
 
 

time: 120 us -> 121 us (level)
  starting transfers between devices: 44.3 us -> 45.7 us
    ppermute x14, starting transfers between devices: 20.9 us -> 22.3 us  [row_shift(): return lax.ppermute(x, 'row', pairs)]
where the time goes in v1:
time: 121 us
  starting transfers between devices  45.7 us (38%)
  waiting for transfers between devices  41.9 us (35%)
  Pallas kernels  29.2 us (24%)
  other arithmetic  2.39 us (2%)
    ppermute x24, waiting for transfers between devices, col_shift(): return lax.ppermute(x, 'col', pairs)  27 us
    ppermute x24, starting transfers between devices, col_shift(): return lax.ppermute(x, 'col', pairs)  23.4 us
    ppermute x14, starting transfers between devices, row_shift(): return lax.ppermute(x, 'row', pairs)  22.3 us
    pallas_call x4, Pallas kernels, call(): pl.pallas_call(kernel, out_shape=[jax.ShapeDtypeStruct(s, F32) for s in o...  20 us
    ppermute x14, waiting for transfers between devices, row_shift(): return lax.ppermute(x, 'row', pairs)  14.8 us
    pallas_call x2, Pallas kernels, pack(): pl.pallas_call(lambda *refs: pack_kernel(begin, end, *refs), out_shape=ja...  9.23 us
  transfers between devices with their start and end apart: 38, of which 12 were waited for; matrix products, arithmetic and copies ran while one was open for 0% of the time, Pallas kernels for 16%

profile of v1, /device:TPU:1, one launch (start us, length us, event | category | flops | bytes accessed | tf_op | source)
XLA Modules:
  0.0 120.8 jit_solution(8918590576859191967)
XLA Ops:
  0.6 3.7 %collective-permute-start.2 = (f32[8,32,256]{2,1,0:T(8,128)}, f32[8,32,256]{2,1,0:T(8,128)S(1)}, u32[]{:S(2)}, u32[]{:S(2)}) collective-permute-start(f32[8,32,256]{2,1,0:T(8,128)} %bitcast.46), channel_id=1, source_target_pairs={{0,16},{16,0},{32,48},{48,32},{64,80},{80,64},{96,112},{112,96},{1... | collective-permute-start | bytes 786440 | tf_op jit(solution)/shard_map/gather_latent/ppermute | solution.py:25
  4.3 2.9 %collective-permute-start.1 = (f32[8,32,256]{2,1,0:T(8,128)}, f32[8,32,256]{2,1,0:T(8,128)S(1)}, u32[]{:S(2)}, u32[]{:S(2)}) collective-permute-start(f32[8,32,256]{2,1,0:T(8,128)} %bitcast.47), channel_id=1, source_target_pairs={{0,64},{16,80},{32,96},{48,112},{64,0},{80,16},{96,32},{112,48},{1... | collective-permute-start | bytes 786440 | tf_op jit(solution)/shard_map/gather_latent/ppermute | solution.py:25
  7.6 2.3 %collective-permute-start.3 = (f32[8,32,256]{2,1,0:T(8,128)}, f32[8,32,256]{2,1,0:T(8,128)S(1)}, u32[]{:S(2)}, u32[]{:S(2)}) collective-permute-start(f32[8,32,256]{2,1,0:T(8,128)} %bitcast.49), channel_id=1, source_target_pairs={{0,96},{16,112},{32,0},{48,16},{64,32},{80,48},{96,64},{112,80},{1... | collective-permute-start | bytes 786440 | tf_op jit(solution)/shard_map/gather_latent/ppermute | solution.py:25
  10.6 4.6 %gather_latent.2.refs_3_ = bf16[72,2,256,256]{3,2,1,0:T(8,128)(2,1)S(1)} custom-call(s32[2]{0:T(128)S(1)} %pad_add_fusion.refs_0_, s32[2,72]{1,0:T(2,128)S(1)} %bitcast.52, f32[1,1,72,256,256]{4,3,2,1,0:T(8,128)} %refs_2_.3), custom_call_target="tpu_custom_call" | custom-call | bytes 18874368 | tf_op jit(solution)/shard_map/gather_latent/pallas_call | solution.py:80
  17.1 4.6 %gather_latent.3.refs_9_ = bf16[72,2,256,256]{3,2,1,0:T(8,128)(2,1)S(1)} custom-call(s32[2]{0:T(128)S(1)} %pad_add_fusion.refs_0_, s32[2,72]{1,0:T(2,128)S(1)} %bitcast.53, f32[1,1,72,256,256]{4,3,2,1,0:T(8,128)} %refs_2_.3, bf16[72,2,256,256]{3,2,1,0:T(8,128)(2,1)S(1)} %gather_latent.2.refs_3_), custom_call_target="tpu_custom_call", output_to_operand_aliasing={{}: (3, {})} | custom-call | bytes 18874368 | tf_op jit(solution)/shard_map/gather_latent/pallas_call | solution.py:80
  24.4 4.8 %field_product.2 = (f32[3,16,16,256]{3,2,1,0:T(8,128)S(1)}, f32[5,16,16,256]{3,2,1,0:T(8,128)S(1)}) custom-call(s32[2]{0:T(128)S(1)} %pad_add_fusion.refs_0_, f32[8,32,256]{2,1,0:T(8,128)S(1)} %bitcast.50, f32[8,32,256]{2,1,0:T(8,128)S(1)} %collective-permute-done.refs_2_, f32[8,32,256]{2,1,0:T(8,128)S(1)} %collective-permute-done.1.refs_3_, ...), custom_call_target="tpu_custom_call" | custom-call | flops 7247757312 | bytes 18874368 | tf_op jit(solution)/shard_map/field_product/pallas_call | solution.py:189
  29.3 2.9 %collective-permute-start.7 = (f32[5,16,16,256]{3,2,1,0:T(8,128)S(1)}, f32[5,16,16,256]{3,2,1,0:T(8,128)S(1)}, u32[]{:S(2)}, u32[]{:S(2)}) collective-permute-start(f32[5,16,16,256]{3,2,1,0:T(8,128)S(1)} %get-tuple-element.48), channel_id=1, source_target_pairs={{0,1},{1,0},{2,3},{3,2},{4,5},{5,4},{6,7},{7,6},{8,9},{9,8},{10,11... | collective-permute-start | bytes 3932168 | tf_op jit(solution)/shard_map/reduce_field/ppermute | solution.py:33
  32.5 4.8 %field_product.3 = (f32[16,16,256]{2,1,0:T(8,128)S(1)}, f32[16,16,256]{2,1,0:T(8,128)S(1)}, f32[16,16,256]{2,1,0:T(8,128)S(1)}, f32[16,16,256]{2,1,0:T(8,128)S(1...) custom-call(s32[2]{0:T(128)S(1)} %pad_add_fusion.refs_0_, ...), custom_call_target="tpu_custom_call" | custom-call | flops 7247757312 | bytes 18874368 | tf_op jit(solution)/shard_map/field_product/pallas_call | solution.py:189
  40.8 2.1 %collective-permute-start.14 = (f32[16,16,256]{2,1,0:T(8,128)S(1)}, f32[16,16,256]{2,1,0:T(8,128)S(1)}, u32[]{:S(2)}, u32[]{:S(2)}) collective-permute-start(f32[16,16,256]{2,1,0:T(8,128)S(1)} %get-tuple-element.63), channel_id=1, source_target_pairs={{0,12},{1,13},{2,14},{3,15},{4,0},{5,1},{6,2},{7,3},{8,4},{9,5},{1... | collective-permute-start | bytes 786440 | tf_op jit(solution)/shard_map/reduce_field/ppermute | solution.py:33
  42.9 2.7 %collective-permute-start.12 = (f32[16,16,256]{2,1,0:T(8,128)S(1)}, f32[16,16,256]{2,1,0:T(8,128)S(1)}, u32[]{:S(2)}, u32[]{:S(2)}) collective-permute-start(f32[16,16,256]{2,1,0:T(8,128)S(1)} %get-tuple-element.60), channel_id=1, source_target_pairs={{0,12},{1,13},{2,14},{3,15},{4,0},{5,1},{6,2},{7,3},{8,4},{9,5},{1... | collective-permute-start | bytes 786440 | tf_op jit(solution)/shard_map/reduce_field/ppermute | solution.py:33
  45.6 3.7 %collective-permute-start.10 = (f32[16,16,256]{2,1,0:T(8,128)S(1)}, f32[16,16,256]{2,1,0:T(8,128)S(1)}, u32[]{:S(2)}, u32[]{:S(2)}) collective-permute-start(f32[16,16,256]{2,1,0:T(8,128)S(1)} %add.84), channel_id=1, source_target_pairs={{0,8},{1,9},{2,10},{3,11},{4,12},{5,13},{6,14},{7,15},{8,0},{9,1},... | collective-permute-start | bytes 786440 | tf_op jit(solution)/shard_map/reduce_field/ppermute | solution.py:33
  50.7 4.0 %collective-permute-done.11 = f32[16,16,256]{2,1,0:T(8,128)S(1)} collective-permute-done((f32[16,16,256]{2,1,0:T(8,128)S(1)}, f32[16,16,256]{2,1,0:T(8,128)S(1)}, u32[]{:S(2)}, u32[]{:S(2)}) %collective-permute-start.11) | collective-permute-done | bytes 262176 | tf_op jit(solution)/shard_map/reduce_field/ppermute | solution.py:33
  54.7 6.5 %collective-permute-done.10 = f32[16,16,256]{2,1,0:T(8,128)S(1)} collective-permute-done((f32[16,16,256]{2,1,0:T(8,128)S(1)}, f32[16,16,256]{2,1,0:T(8,128)S(1)}, u32[]{:S(2)}, u32[]{:S(2)}) %collective-permute-start.10) | collective-permute-done | bytes 262176 | tf_op jit(solution)/shard_map/reduce_field/ppermute | solution.py:33
  65.2 3.2 %collective-permute-done.16.refs_5_ = f32[16,16,256]{2,1,0:T(8,128)S(1)} collective-permute-done((f32[16,16,256]{2,1,0:T(8,128)S(1)}, f32[16,16,256]{2,1,0:T(8,128)S(1)}, u32[]{:S(2)}, u32[]{:S(2)}) %collective-permute-start.16) | collective-permute-done | bytes 262176 | tf_op jit(solution)/shard_map/gather_slope/ppermute | solution.py:33
  71.3 6.2 %collective-permute-done.17.refs_2_ = f32[16,16,256]{2,1,0:T(8,128)S(1)} collective-permute-done((f32[16,16,256]{2,1,0:T(8,128)S(1)}, f32[16,16,256]{2,1,0:T(8,128)S(1)}, u32[]{:S(2)}, u32[]{:S(2)}) %collective-permute-start.17) | collective-permute-done | bytes 262176 | tf_op jit(solution)/shard_map/gather_slope/ppermute | solution.py:33
  77.5 5.6 %collective-permute-done.20.refs_6_ = f32[16,16,256]{2,1,0:T(8,128)S(1)} collective-permute-done((f32[16,16,256]{2,1,0:T(8,128)S(1)}, f32[16,16,256]{2,1,0:T(8,128)S(1)}, u32[]{:S(2)}, u32[]{:S(2)}) %collective-permute-start.20) | collective-permute-done | bytes 262176 | tf_op jit(solution)/shard_map/gather_slope/ppermute | solution.py:33
  86.0 5.0 %gradient_product.2.refs_10_ = f32[8,256,256]{2,1,0:T(8,128)S(1)} custom-call(s32[2]{0:T(128)S(1)} %pad_add_fusion.refs_0_, f32[16,16,256]{2,1,0:T(8,128)S(1)} %get-tuple-element.65.refs_1_, f32[16,16,256]{2,1,0:T(8,128)S(1)} %collective-permute-done.17.refs_2_, f32[16,16,256]{2,1,0:T(8,128)S(1)} %collective-permute-done.19.refs_3_, ...), custom_call_target="tpu_custom_call" | custom-call | flops 7247757312 | bytes 18874368 | tf_op jit(solution)/shard_map/gradient_product/pallas_call | solution.py:189
  91.0 5.4 %gradient_product.3 = (f32[8,32,256]{2,1,0:T(8,128)S(1)}, f32[4,32,256]{2,1,0:T(8,128)S(1)}, f32[8,32,256]{2,1,0:T(8,128)S(1)}, f32[4,32,256]{2,1,0:T(8,128)S(1)...) custom-call(s32[2]{0:T(128)S(1)} %pad_add_fusion.refs_0_, ...), custom_call_target="tpu_custom_call" | custom-call | flops 7247757312 | bytes 18874368 | tf_op jit(solution)/shard_map/gradient_product/pallas_call | solution.py:189
  96.6 2.6 %collective-permute-start.35 = (f32[12,32,256]{2,1,0:T(8,128)S(1)}, f32[12,32,256]{2,1,0:T(8,128)S(1)}, u32[]{:S(2)}, u32[]{:S(2)}) collective-permute-start(f32[12,32,256]{2,1,0:T(8,128)S(1)} %get-tuple-element.77), channel_id=1, source_target_pairs={{0,96},{16,112},{32,0},{48,16},{64,32},{80,48},{96,64},{112,80},{1... | collective-permute-start | bytes 1179656 | tf_op jit(solution)/shard_map/reduce_gradient/ppermute | solution.py:25
  99.2 2.8 %collective-permute-start.31 = (f32[8,32,256]{2,1,0:T(8,128)S(1)}, f32[8,32,256]{2,1,0:T(8,128)S(1)}, u32[]{:S(2)}, u32[]{:S(2)}) collective-permute-start(f32[8,32,256]{2,1,0:T(8,128)S(1)} %get-tuple-element.74), channel_id=1, source_target_pairs={{0,16},{16,0},{32,48},{48,32},{64,80},{80,64},{96,112},{112,96},{1... | collective-permute-start | bytes 786440 | tf_op jit(solution)/shard_map/reduce_gradient/ppermute | solution.py:25
  101.9 5.9 %collective-permute-done.31 = f32[8,32,256]{2,1,0:T(8,128)S(1)} collective-permute-done((f32[8,32,256]{2,1,0:T(8,128)S(1)}, f32[8,32,256]{2,1,0:T(8,128)S(1)}, u32[]{:S(2)}, u32[]{:S(2)}) %collective-permute-start.31) | collective-permute-done | bytes 262176 | tf_op jit(solution)/shard_map/reduce_gradient/ppermute | solution.py:25
  108.3 2.8 %collective-permute-start.37 = (f32[8,32,256]{2,1,0:T(8,128)S(1)}, f32[8,32,256]{2,1,0:T(8,128)S(1)}, u32[]{:S(2)}, u32[]{:S(2)}) collective-permute-start(f32[8,32,256]{2,1,0:T(8,128)S(1)} %slice_add_fusion), channel_id=1, source_target_pairs={{0,16},{16,0},{32,48},{48,32},{64,80},{80,64},{96,112},{112,96},{1... | collective-permute-start | bytes 786440 | tf_op jit(solution)/shard_map/reduce_gradient/ppermute | solution.py:25
  111.7 2.1 %collective-permute-start.36 = (f32[4,32,256]{2,1,0:T(8,128)S(1)}, f32[4,32,256]{2,1,0:T(8,128)S(1)}, u32[]{:S(2)}, u32[]{:S(2)}) collective-permute-start(f32[4,32,256]{2,1,0:T(8,128)S(1)} %get-tuple-element.78), channel_id=1, source_target_pairs={{0,96},{16,112},{32,0},{48,16},{64,32},{80,48},{96,64},{112,80},{1... | collective-permute-start | bytes 393224 | tf_op jit(solution)/shard_map/reduce_gradient/ppermute | solution.py:25
  113.9 6.1 %collective-permute-done.34 = f32[4,32,256]{2,1,0:T(8,128)S(1)} collective-permute-done((f32[4,32,256]{2,1,0:T(8,128)S(1)}, f32[4,32,256]{2,1,0:T(8,128)S(1)}, u32[]{:S(2)}, u32[]{:S(2)}) %collective-permute-start.34) | collective-permute-done | bytes 131104 | tf_op jit(solution)/shard_map/reduce_gradient/ppermute | solution.py:25
  (77 shorter events, 22.7 us)
Async XLA Ops:
  0.6 14.7 %collective-permute-start.2 = (f32[8,32,256]{2,1,0:T(8,128)}, f32[8,32,256]{2,1,0:T(8,128)S(1)}, u32[]{:S(2)}, u32[]{:S(2)}) collective-permute-start(f32[8,32,256]{2,1,0:T(8,128)} %bitcast.46), channel_id=1, source_target_pairs={{0,16},{16,0},{32,48},{48,32},{64,80},{80,64},{96,112},{112,96},{1... | collective-permute-start | bytes 786440 | tf_op jit(solution)/shard_map/gather_latent/ppermute | solution.py:25
  4.3 11.0 %collective-permute-start.1 = (f32[8,32,256]{2,1,0:T(8,128)}, f32[8,32,256]{2,1,0:T(8,128)S(1)}, u32[]{:S(2)}, u32[]{:S(2)}) collective-permute-start(f32[8,32,256]{2,1,0:T(8,128)} %bitcast.47), channel_id=1, source_target_pairs={{0,64},{16,80},{32,96},{48,112},{64,0},{80,16},{96,32},{112,48},{1... | collective-permute-start | bytes 786440 | tf_op jit(solution)/shard_map/gather_latent/ppermute | solution.py:25
  7.2 14.5 %collective-permute-start = (f32[8,32,256]{2,1,0:T(8,128)}, f32[8,32,256]{2,1,0:T(8,128)S(1)}, u32[]{:S(2)}, u32[]{:S(2)}) collective-permute-start(f32[8,32,256]{2,1,0:T(8,128)} %bitcast.48), channel_id=1, source_target_pairs={{0,32},{16,48},{32,64},{48,80},{64,96},{80,112},{96,0},{112,16},{1... | collective-permute-start | bytes 786440 | tf_op jit(solution)/shard_map/gather_latent/ppermute | solution.py:25
  7.6 14.1 %collective-permute-start.3 = (f32[8,32,256]{2,1,0:T(8,128)}, f32[8,32,256]{2,1,0:T(8,128)S(1)}, u32[]{:S(2)}, u32[]{:S(2)}) collective-permute-start(f32[8,32,256]{2,1,0:T(8,128)} %bitcast.49), channel_id=1, source_target_pairs={{0,96},{16,112},{32,0},{48,16},{64,32},{80,48},{96,64},{112,80},{1... | collective-permute-start | bytes 786440 | tf_op jit(solution)/shard_map/gather_latent/ppermute | solution.py:25
  15.6 8.8 %collective-permute-start.6 = (f32[8,32,256]{2,1,0:T(8,128)S(1)}, f32[8,32,256]{2,1,0:T(8,128)S(1)}, u32[]{:S(2)}, u32[]{:S(2)}) collective-permute-start(f32[8,32,256]{2,1,0:T(8,128)S(1)} %collective-permute-done.2.refs_5_), channel_id=1, source_target_pairs={{0,96},{16,112},{32,0},{48,16},{64,32},{80,48},{96,64},{112,80},{1... | collective-permute-start | bytes 786440 | tf_op jit(solution)/shard_map/gather_latent/ppermute | solution.py:25
  15.9 8.5 %collective-permute-start.4 = (f32[8,32,256]{2,1,0:T(8,128)S(1)}, f32[8,32,256]{2,1,0:T(8,128)S(1)}, u32[]{:S(2)}, u32[]{:S(2)}) collective-permute-start(f32[8,32,256]{2,1,0:T(8,128)S(1)} %collective-permute-done.2.refs_5_), channel_id=1, source_target_pairs={{0,32},{16,48},{32,64},{48,80},{64,96},{80,112},{96,0},{112,16},{1... | collective-permute-start | bytes 786440 | tf_op jit(solution)/shard_map/gather_latent/ppermute | solution.py:25
  39.1 10.2 %collective-permute-start.13 = (f32[16,16,256]{2,1,0:T(8,128)S(1)}, f32[16,16,256]{2,1,0:T(8,128)S(1)}, u32[]{:S(2)}, u32[]{:S(2)}) collective-permute-start(f32[16,16,256]{2,1,0:T(8,128)S(1)} %get-tuple-element.62), channel_id=1, source_target_pairs={{0,4},{1,5},{2,6},{3,7},{4,8},{5,9},{6,10},{7,11},{8,12},{9,13},{1... | collective-permute-start | bytes 786440 | tf_op jit(solution)/shard_map/reduce_field/ppermute | solution.py:33
  40.8 8.5 %collective-permute-start.14 = (f32[16,16,256]{2,1,0:T(8,128)S(1)}, f32[16,16,256]{2,1,0:T(8,128)S(1)}, u32[]{:S(2)}, u32[]{:S(2)}) collective-permute-start(f32[16,16,256]{2,1,0:T(8,128)S(1)} %get-tuple-element.63), channel_id=1, source_target_pairs={{0,12},{1,13},{2,14},{3,15},{4,0},{5,1},{6,2},{7,3},{8,4},{9,5},{1... | collective-permute-start | bytes 786440 | tf_op jit(solution)/shard_map/reduce_field/ppermute | solution.py:33
  42.9 11.8 %collective-permute-start.11 = (f32[16,16,256]{2,1,0:T(8,128)S(1)}, f32[16,16,256]{2,1,0:T(8,128)S(1)}, u32[]{:S(2)}, u32[]{:S(2)}) collective-permute-start(f32[16,16,256]{2,1,0:T(8,128)S(1)} %get-tuple-element.59), channel_id=1, source_target_pairs={{0,4},{1,5},{2,6},{3,7},{4,8},{5,9},{6,10},{7,11},{8,12},{9,13},{1... | collective-permute-start | bytes 786440 | tf_op jit(solution)/shard_map/reduce_field/ppermute | solution.py:33
  42.9 11.8 %collective-permute-start.12 = (f32[16,16,256]{2,1,0:T(8,128)S(1)}, f32[16,16,256]{2,1,0:T(8,128)S(1)}, u32[]{:S(2)}, u32[]{:S(2)}) collective-permute-start(f32[16,16,256]{2,1,0:T(8,128)S(1)} %get-tuple-element.60), channel_id=1, source_target_pairs={{0,12},{1,13},{2,14},{3,15},{4,0},{5,1},{6,2},{7,3},{8,4},{9,5},{1... | collective-permute-start | bytes 786440 | tf_op jit(solution)/shard_map/reduce_field/ppermute | solution.py:33
  45.6 15.6 %collective-permute-start.10 = (f32[16,16,256]{2,1,0:T(8,128)S(1)}, f32[16,16,256]{2,1,0:T(8,128)S(1)}, u32[]{:S(2)}, u32[]{:S(2)}) collective-permute-start(f32[16,16,256]{2,1,0:T(8,128)S(1)} %add.84), channel_id=1, source_target_pairs={{0,8},{1,9},{2,10},{3,11},{4,12},{5,13},{6,14},{7,15},{8,0},{9,1},... | collective-permute-start | bytes 786440 | tf_op jit(solution)/shard_map/reduce_field/ppermute | solution.py:33
  49.4 11.8 %collective-permute-start.15 = (f32[16,16,256]{2,1,0:T(8,128)S(1)}, f32[16,16,256]{2,1,0:T(8,128)S(1)}, u32[]{:S(2)}, u32[]{:S(2)}) collective-permute-start(f32[16,16,256]{2,1,0:T(8,128)S(1)} %add_add_fusion), channel_id=1, source_target_pairs={{0,2},{1,3},{2,0},{3,1},{4,6},{5,7},{6,4},{7,5},{8,10},{9,11},{10,... | collective-permute-start | bytes 786440 | tf_op jit(solution)/shard_map/reduce_field/ppermute | solution.py:33
  62.2 15.3 %collective-permute-start.17 = (f32[16,16,256]{2,1,0:T(8,128)S(1)}, f32[16,16,256]{2,1,0:T(8,128)S(1)}, u32[]{:S(2)}, u32[]{:S(2)}) collective-permute-start(f32[16,16,256]{2,1,0:T(8,128)S(1)} %get-tuple-element.65.refs_1_), channel_id=1, source_target_pairs={{0,4},{1,5},{2,6},{3,7},{4,8},{5,9},{6,10},{7,11},{8,12},{9,13},{1... | collective-permute-start | bytes 786440 | tf_op jit(solution)/shard_map/gather_slope/ppermute | solution.py:33
  63.5 14.0 %collective-permute-start.18 = (f32[16,16,256]{2,1,0:T(8,128)S(1)}, f32[16,16,256]{2,1,0:T(8,128)S(1)}, u32[]{:S(2)}, u32[]{:S(2)}) collective-permute-start(f32[16,16,256]{2,1,0:T(8,128)S(1)} %get-tuple-element.65.refs_1_), channel_id=1, source_target_pairs={{0,12},{1,13},{2,14},{3,15},{4,0},{5,1},{6,2},{7,3},{8,4},{9,5},{1... | collective-permute-start | bytes 786440 | tf_op jit(solution)/shard_map/gather_slope/ppermute | solution.py:33
  68.4 14.7 %collective-permute-start.20 = (f32[16,16,256]{2,1,0:T(8,128)S(1)}, f32[16,16,256]{2,1,0:T(8,128)S(1)}, u32[]{:S(2)}, u32[]{:S(2)}) collective-permute-start(f32[16,16,256]{2,1,0:T(8,128)S(1)} %collective-permute-done.16.refs_5_), channel_id=1, source_target_pairs={{0,4},{1,5},{2,6},{3,7},{4,8},{5,9},{6,10},{7,11},{8,12},{9,13},{1... | collective-permute-start | bytes 786440 | tf_op jit(solution)/shard_map/gather_slope/ppermute | solution.py:33
  70.0 14.2 %collective-permute-start.27 = (f32[16,16,256]{2,1,0:T(8,128)S(1)}, f32[16,16,256]{2,1,0:T(8,128)S(1)}, u32[]{:S(2)}, u32[]{:S(2)}) collective-permute-start(f32[16,16,256]{2,1,0:T(8,128)S(1)} %collective-permute-done.19.refs_3_), channel_id=1, source_target_pairs={{0,2},{1,3},{2,0},{3,1},{4,6},{5,7},{6,4},{7,5},{8,10},{9,11},{10,... | collective-permute-start | bytes 786440 | tf_op jit(solution)/shard_map/gather_slope/ppermute | solution.py:33
  71.2 13.0 %collective-permute-start.29 = (f32[16,16,256]{2,1,0:T(8,128)S(1)}, f32[16,16,256]{2,1,0:T(8,128)S(1)}, u32[]{:S(2)}, u32[]{:S(2)}) collective-permute-start(f32[16,16,256]{2,1,0:T(8,128)S(1)} %collective-permute-done.16.refs_5_), channel_id=1, source_target_pairs={{0,12},{1,13},{2,14},{3,15},{4,0},{5,1},{6,2},{7,3},{8,4},{9,5},{1... | collective-permute-start | bytes 786440 | tf_op jit(solution)/shard_map/gather_slope/ppermute | solution.py:33
  96.4 11.9 %collective-permute-start.33 = (f32[12,32,256]{2,1,0:T(8,128)S(1)}, f32[12,32,256]{2,1,0:T(8,128)S(1)}, u32[]{:S(2)}, u32[]{:S(2)}) collective-permute-start(f32[12,32,256]{2,1,0:T(8,128)S(1)} %get-tuple-element.75), channel_id=1, source_target_pairs={{0,32},{16,48},{32,64},{48,80},{64,96},{80,112},{96,0},{112,16},{1... | collective-permute-start | bytes 1179656 | tf_op jit(solution)/shard_map/reduce_gradient/ppermute | solution.py:25
  96.6 11.7 %collective-permute-start.35 = (f32[12,32,256]{2,1,0:T(8,128)S(1)}, f32[12,32,256]{2,1,0:T(8,128)S(1)}, u32[]{:S(2)}, u32[]{:S(2)}) collective-permute-start(f32[12,32,256]{2,1,0:T(8,128)S(1)} %get-tuple-element.77), channel_id=1, source_target_pairs={{0,96},{16,112},{32,0},{48,16},{64,32},{80,48},{96,64},{112,80},{1... | collective-permute-start | bytes 1179656 | tf_op jit(solution)/shard_map/reduce_gradient/ppermute | solution.py:25
  99.2 8.6 %collective-permute-start.31 = (f32[8,32,256]{2,1,0:T(8,128)S(1)}, f32[8,32,256]{2,1,0:T(8,128)S(1)}, u32[]{:S(2)}, u32[]{:S(2)}) collective-permute-start(f32[8,32,256]{2,1,0:T(8,128)S(1)} %get-tuple-element.74), channel_id=1, source_target_pairs={{0,16},{16,0},{32,48},{48,32},{64,80},{80,64},{96,112},{112,96},{1... | collective-permute-start | bytes 786440 | tf_op jit(solution)/shard_map/reduce_gradient/ppermute | solution.py:25
  107.8 12.1 %collective-permute-start.32 = (f32[8,32,256]{2,1,0:T(8,128)S(1)}, f32[8,32,256]{2,1,0:T(8,128)S(1)}, u32[]{:S(2)}, u32[]{:S(2)}) collective-permute-start(f32[8,32,256]{2,1,0:T(8,128)S(1)} %add.94), channel_id=1, source_target_pairs={{0,64},{16,80},{32,96},{48,112},{64,0},{80,16},{96,32},{112,48},{1... | collective-permute-start | bytes 786440 | tf_op jit(solution)/shard_map/reduce_gradient/ppermute | solution.py:25
  108.3 11.6 %collective-permute-start.37 = (f32[8,32,256]{2,1,0:T(8,128)S(1)}, f32[8,32,256]{2,1,0:T(8,128)S(1)}, u32[]{:S(2)}, u32[]{:S(2)}) collective-permute-start(f32[8,32,256]{2,1,0:T(8,128)S(1)} %slice_add_fusion), channel_id=1, source_target_pairs={{0,16},{16,0},{32,48},{48,32},{64,80},{80,64},{96,112},{112,96},{1... | collective-permute-start | bytes 786440 | tf_op jit(solution)/shard_map/reduce_gradient/ppermute | solution.py:25
  111.2 8.8 %collective-permute-start.34 = (f32[4,32,256]{2,1,0:T(8,128)S(1)}, f32[4,32,256]{2,1,0:T(8,128)S(1)}, u32[]{:S(2)}, u32[]{:S(2)}) collective-permute-start(f32[4,32,256]{2,1,0:T(8,128)S(1)} %get-tuple-element.76), channel_id=1, source_target_pairs={{0,32},{16,48},{32,64},{48,80},{64,96},{80,112},{96,0},{112,16},{1... | collective-permute-start | bytes 393224 | tf_op jit(solution)/shard_map/reduce_gradient/ppermute | solution.py:25
  111.7 8.2 %collective-permute-start.36 = (f32[4,32,256]{2,1,0:T(8,128)S(1)}, f32[4,32,256]{2,1,0:T(8,128)S(1)}, u32[]{:S(2)}, u32[]{:S(2)}) collective-permute-start(f32[4,32,256]{2,1,0:T(8,128)S(1)} %get-tuple-element.78), channel_id=1, source_target_pairs={{0,96},{16,112},{32,0},{48,16},{64,32},{80,48},{96,64},{112,80},{1... | collective-permute-start | bytes 393224 | tf_op jit(solution)/shard_map/reduce_gradient/ppermute | solution.py:25
  (18 other events, 125.7 us)
